TPU v7x, 32 devices: a whole 2x2x4 slice. The times are simulated.
32 devices in a mesh: ka: 2 (over core), ga: 16 (over z, y, x).
Axes of the slice: x: 2, y: 2, z: 4, core: 2. Of those that a mesh axis runs over, the one named last changes fastest.
Arguments:
- wavefunctions: bfloat16 [16, 2, 16, 32, 256], P('ka', None, None, 'ga'), may hold values from -6 to 6
- partner: int32 [16], replicated, may hold values from 0 to 15, each once
- gmap: int32 [8192], replicated, may hold values from 0 to 8191, as said below
- screened: bfloat16 [8192, 8192], P('ga'), may hold values from -0.0007324219 to 0.0007324219
Outputs:
- kernel_rows: float32 [16, 2, 4096], P('ka')
- kernel_mirror: float32 [16, 2, 4096], P('ka')
Inputs may be any that keep to these rules, and one draw needn't show every extreme that they name: `partner`: each k-point appears exactly once. Entries j and gmap[j] lie in the same aligned block of 32; within each block every index appears once.
All inputs are finite; a program needn't handle non-finite values.
Results may differ from a plain program's by a relative error of at most 0.0042.
Values may be sent and summed in bfloat16 or wider, within the bound.
A program may use at most 256 MiB of HBM per device.

v0:
```python
import functools
import math

import jax
import jax.numpy as jnp
import numpy as np
from jax import lax
from jax.experimental import pallas as pl
from jax.experimental.pallas import tpu as pltpu
from jax.sharding import PartitionSpec as P

NV = 8
NC = 8
NX = 16
NY = 16
NZ = 32
NXY = NX * NY
NG = NXY * NZ
PAIRS = 64
GROUP = 256
STEP_Z = 8
BF = jnp.bfloat16
F32 = jnp.float32
VMEM_LIMIT = 56 * 1024 * 1024
SCALE_16 = 1.1329
SCALE_32 = 1.6245


def split(values):
    high = values.astype(BF)
    return high, (values - high.astype(F32)).astype(BF)


def line_table():
    z = np.arange(NZ)
    angle = -2.0 * np.pi * (z[:, None] * z[None, :] % NZ) / NZ
    return SCALE_32 * np.concatenate([np.cos(angle), np.sin(angle)], axis=0)


def plane_table():
    r = np.arange(NXY)
    x, y = r // NY, r % NY
    turns = (x[:, None] * x[None, :] % NX) / NX + (y[:, None] * y[None, :] % NY) / NY
    c, s = np.cos(-2.0 * np.pi * turns), np.sin(-2.0 * np.pi * turns)
    return SCALE_16 * np.block([[c, -s], [s, c]])


def interaction_kernel(steps, line_ref, plane_ref, gz_ref, w_ref, out_ref, mid_ref, low_ref):
    step = pl.program_id(0)
    rows = w_ref.shape[0]
    per = w_ref.shape[1] // GROUP
    cols = GROUP // NZ

    @pl.when(step < steps)
    def _():
        parts = []
        for g in range(per):
            gz = gz_ref[0, :, g * GROUP : (g + 1) * GROUP]
            hot = lax.broadcasted_iota(jnp.int32, (NZ, GROUP), 0) == gz
            table = jnp.dot(line_ref[...], hot.astype(F32).astype(BF), preferred_element_type=F32)
            column = lax.broadcasted_iota(jnp.int32, (cols, GROUP), 1) // NZ
            mask = column == lax.broadcasted_iota(jnp.int32, (cols, GROUP), 0)
            wide = jnp.where(mask[None], table[:, None, :], 0.0)
            wide = wide.reshape(2 * NZ * cols, GROUP).astype(BF)
            got = lax.dot_general(
                wide,
                w_ref[:, g * GROUP : (g + 1) * GROUP],
                (((1,), (1,)), ((), ())),
                preferred_element_type=F32,
            )
            parts.append(got.reshape(2, NZ, cols, rows))
        high, low = split(jnp.concatenate(parts, axis=2))
        start = pl.multiple_of(step * (per * cols), per * cols)
        for p in range(2):
            mid_ref[:, p, pl.ds(start, per * cols), :] = high[p]
            low_ref[:, p, pl.ds(start, per * cols), :] = low[p]

    @pl.when(step >= steps)
    def _():
        planes = out_ref.shape[0]
        for i in range(planes):
            z = (step - steps) * planes + i
            mid = mid_ref[z].reshape(2 * NXY, rows)
            low = low_ref[z].reshape(2 * NXY, rows)
            got = jnp.dot(plane_ref[...], mid, preferred_element_type=F32)
            got = (got + jnp.dot(plane_ref[...], low, preferred_element_type=F32)).astype(BF)
            out_ref[i, :, :rows] = got[:NXY]
            out_ref[i, :, rows:] = got[NXY:]


def transformed_interaction(gmap, screened):
    rows = screened.shape[0]
    per = 2
    steps = NG // (GROUP * per)
    planes = 2
    gz = (gmap % NZ).reshape(steps, 1, GROUP * per)
    last = steps - 1
    return pl.pallas_call(
        functools.partial(interaction_kernel, steps),
        grid=(steps + NZ // planes,),
        in_specs=[
            pl.BlockSpec((2 * NZ, NZ), lambda i: (0, 0)),
            pl.BlockSpec((2 * NXY, 2 * NXY), lambda i: (0, 0)),
            pl.BlockSpec((1, 1, GROUP * per), lambda i: (jnp.minimum(i, last), 0, 0)),
            pl.BlockSpec((rows, GROUP * per), lambda i: (0, jnp.minimum(i, last))),
        ],
        out_specs=pl.BlockSpec(
            (planes, NXY, 2 * rows), lambda i: (jnp.maximum(i - steps, 0), 0, 0)
        ),
        out_shape=jax.ShapeDtypeStruct((NZ, NXY, 2 * rows), BF),
        scratch_shapes=[pltpu.VMEM((NZ, 2, NXY, rows), BF)] * 2,
        compiler_params=pltpu.CompilerParams(vmem_limit_bytes=VMEM_LIMIT),
        cost_estimate=pl.CostEstimate(
            flops=16 * NXY * NG * rows, bytes_accessed=6 * NG * rows, transcendentals=0
        ),
    )(jnp.asarray(line_table(), BF), jnp.asarray(plane_table(), BF), gz, screened)


def pair_rows(left, right):
    left_real, left_imag = left
    right_real, right_imag = right
    real_part = [
        left_real[b : b + 1] * right_real + left_imag[b : b + 1] * right_imag for b in range(8)
    ]
    imag_part = [
        left_real[b : b + 1] * right_imag - left_imag[b : b + 1] * right_real for b in range(8)
    ]
    return (
        jnp.concatenate(real_part, axis=0),
        jnp.concatenate(imag_part, axis=0),
    )


def contraction_kernel(
    pairs,
    who_ref,
    waves_ref,
    inter_ref,
    first_ref,
    second_ref,
    out_ref,
    val_ref,
    cond_ref,
    cond_low_ref,
    response_ref,
    spectrum_ref,
):
    step = pl.program_id(0)
    half = pairs * PAIRS
    rows = response_ref.shape[1] // 2

    def fill(k, carry):
        for z in range(STEP_Z):
            home = waves_ref[who_ref[0], z, k].astype(F32)
            away = waves_ref[who_ref[1 + k], z, who_ref[1 + pairs + k]].astype(F32)
            for first in (0, NV):
                left = (home[0, first : first + 8], home[1, first : first + 8])
                right = (away[0, first : first + 8], away[1, first : first + 8])
                real_part, imag_part = pair_rows(left, right)
                start = pl.multiple_of(k * PAIRS, PAIRS)
                lanes = slice(z * NXY, (z + 1) * NXY)
                if first == 0:
                    val_ref[pl.ds(start, PAIRS), lanes] = real_part.astype(BF)
                    val_ref[pl.ds(half + start, PAIRS), lanes] = imag_part.astype(BF)
                else:
                    high, low = split(real_part)
                    cond_ref[pl.ds(start, PAIRS), lanes] = high
                    cond_low_ref[pl.ds(start, PAIRS), lanes] = low
                    high, low = split(imag_part)
                    cond_ref[pl.ds(half + start, PAIRS), lanes] = high
                    cond_low_ref[pl.ds(half + start, PAIRS), lanes] = low
        return carry

    lax.fori_loop(0, pairs, fill, 0)

    @pl.when(step == 0)
    def _():
        response_ref[...] = jnp.zeros_like(response_ref)
        spectrum_ref[...] = jnp.zeros_like(spectrum_ref)

    inter = inter_ref[...].reshape(STEP_Z * NXY, 2 * rows)
    response_ref[...] += jnp.dot(val_ref[...], inter, preferred_element_type=F32)
    mixed = jnp.dot(cond_ref[...], first_ref[...], preferred_element_type=F32)
    mixed = mixed + jnp.dot(cond_low_ref[...], first_ref[...], preferred_element_type=F32)
    mixed, mixed_low = split(mixed)
    spectrum_ref[...] += jnp.dot(mixed, second_ref[0], preferred_element_type=F32) + jnp.dot(
        mixed_low, second_ref[0], preferred_element_type=F32
    )

    @pl.when(step == pl.num_programs(0) - 1)
    def _():
        def finish(k, carry):
            start = pl.multiple_of(k * PAIRS, PAIRS)
            top = pl.ds(start, PAIRS)
            low = pl.ds(half + start, PAIRS)

            def whole(ref):
                real_part = ref[top, :rows] - ref[low, rows:]
                imag_part = ref[top, rows:] + ref[low, :rows]
                return split(jnp.concatenate([real_part, imag_part], axis=0))

            def mixed_product(left, right):
                return lax.dot_general(
                    left, right, (((1,), (1,)), ((), ())), preferred_element_type=F32
                )

            cond, cond_low = whole(spectrum_ref)
            resp, resp_low = whole(response_ref)
            product = mixed_product(cond, resp)
            product = product + mixed_product(cond_low, resp) + mixed_product(cond, resp_low)
            scale = 1.0 / (NG * (SCALE_16 * SCALE_32) ** 2)
            a, b = product[:PAIRS], product[PAIRS:]
            out_ref[k, 0] = (a[:, :PAIRS] + b[:, PAIRS:]) * scale
            out_ref[k, 1] = (a[:, PAIRS:] - b[:, :PAIRS]) * scale
            return carry

        lax.fori_loop(0, pairs, finish, 0)


def partial_kernel(who, waves, inter, first, second):
    holders, _, pairs = waves.shape[:3]
    rows2 = inter.shape[2]
    half2 = 2 * pairs * PAIRS
    steps = NZ // STEP_Z
    spec = pltpu.PrefetchScalarGridSpec(
        num_scalar_prefetch=1,
        grid=(steps,),
        in_specs=[
            pl.BlockSpec(
                (holders, STEP_Z, pairs, 2, NV + NC, NXY), lambda i, who: (0, i, 0, 0, 0, 0)
            ),
            pl.BlockSpec((STEP_Z, NXY, rows2), lambda i, who: (i, 0, 0)),
            pl.BlockSpec(first.shape, lambda i, who: (0, 0)),
            pl.BlockSpec((1,) + second.shape[1:], lambda i, who: (i, 0, 0)),
        ],
        out_specs=pl.BlockSpec((pairs, 2, PAIRS, PAIRS), lambda i, who: (0, 0, 0, 0)),
        scratch_shapes=[
            pltpu.VMEM((half2, STEP_Z * NXY), BF),
            pltpu.VMEM((half2, STEP_Z * NXY), BF),
            pltpu.VMEM((half2, STEP_Z * NXY), BF),
            pltpu.VMEM((half2, rows2), F32),
            pltpu.VMEM((half2, rows2), F32),
        ],
    )
    return pl.pallas_call(
        functools.partial(contraction_kernel, pairs),
        grid_spec=spec,
        out_shape=jax.ShapeDtypeStruct((pairs, 2, PAIRS, PAIRS), F32),
        compiler_params=pltpu.CompilerParams(vmem_limit_bytes=VMEM_LIMIT),
        cost_estimate=pl.CostEstimate(
            flops=2 * half2 * rows2 * NG, bytes_accessed=2 * inter.size, transcendentals=0
        ),
    )(who, waves, inter, first, second)


def local_tables(gmap, place, rows):
    columns = rows // NZ
    number = place * columns + jnp.arange(columns, dtype=jnp.int32)
    gx, gy = number // NY, number % NY
    r = jnp.arange(NXY, dtype=jnp.int32)
    turns = ((r // NY)[:, None] * gx[None] + (r % NY)[:, None] * gy[None]) % NX
    angle = turns.astype(F32) * (-2.0 * math.pi / NX)
    plane = SCALE_16 * jnp.stack([jnp.cos(angle), jnp.sin(angle)], axis=1)
    same = jnp.asarray(np.eye(STEP_Z), F32)
    first = same[:, None, :, None, None] * plane[None, :, None]
    first = first.reshape(STEP_Z * NXY, STEP_Z * 2 * columns).astype(BF)
    gz = lax.dynamic_slice_in_dim(gmap, place * rows, rows) % NZ
    z = jnp.arange(NZ, dtype=jnp.int32)
    angle = (z[:, None] * gz[None] % NZ).astype(F32) * (-2.0 * math.pi / NZ)
    c, s = SCALE_32 * jnp.cos(angle), SCALE_32 * jnp.sin(angle)
    line = jnp.stack([jnp.stack([c, s], axis=1), jnp.stack([-s, c], axis=1)], axis=1)
    own = (jnp.arange(rows) // NZ)[None, :] == jnp.arange(columns)[:, None]
    second = jnp.where(own[None, None, :, None, :], line[:, :, None], 0.0)
    second = second.reshape(NZ // STEP_Z, STEP_Z * 2 * columns, 2 * rows).astype(BF)
    return first, second


def swap_blocks(blocks):
    number = blocks.shape[0]
    moved = (
        blocks.reshape(number, 2, NC, NC, NV, NV)
        .transpose(0, 1, 3, 2, 5, 4)
        .reshape(number, 2, NC * NC * NV * NV)
    )
    return moved * jnp.array([1.0, -1.0], dtype=F32)[None, :, None]


def on_device(wavefunctions, partner, gmap, screened):
    pairs = wavefunctions.shape[0]
    ka_place = lax.axis_index("ka")
    ga_place = lax.axis_index("ga")
    owned = ka_place * pairs + jnp.arange(pairs, dtype=jnp.int32)
    wanted = partner[owned]
    waves = lax.all_gather(wavefunctions.transpose(3, 0, 1, 2, 4), "ga", axis=0, tiled=True)
    waves = lax.all_gather(waves, "ka", axis=0)
    inter = transformed_interaction(gmap, screened)
    first, second = local_tables(gmap, ga_place, screened.shape[0])
    who = jnp.concatenate([ka_place[None].astype(jnp.int32), wanted // pairs, wanted % pairs])
    part = partial_kernel(who, waves, inter, first, second)
    summed = lax.psum(part.reshape(pairs, 2, NC * NC * NV * NV), "ga")
    everyone = lax.all_gather(summed, "ka", axis=0, tiled=True)
    source = jnp.sum(
        jnp.where(
            partner[None, :] == owned[:, None],
            jnp.arange(partner.shape[0], dtype=jnp.int32)[None],
            0,
        ),
        axis=1,
    )
    mirror_out = swap_blocks(jnp.take(everyone, source, axis=0))
    return (summed, mirror_out)


def solution(mesh):
    in_specs = (P("ka", None, None, "ga", None), P(), P(), P("ga", None))
    out_specs = (P("ka", None, None), P("ka", None, None))
    return jax.shard_map(
        on_device, mesh=mesh, in_specs=in_specs, out_specs=out_specs, check_vma=False
    )
```

profile of v0, /device:TPU:0, one launch (start us, length us, event | category | flops | bytes accessed | tf_op | source)
XLA Modules:
  0.0 342.0 jit_solution(8727240353672907993)
XLA Ops:
  7.2 0.0 copy-start.3
  7.2 0.0 copy-start.2
  7.2 0.0 all-gather.4.cloned.1.call-start
  7.2 1.7 copy.35
  8.9 0.0 all-gather.4.cloned.1.call-update
  8.9 0.0 all-gather.6.cloned.1.call-start
  9.0 81.2 %all-gather.4.cloned.1.call-done = bf16[32,8,2,16,256]{4,3,2,1,0:T(8,128)(2,1)} async-done(((bf16[2,8,2,16,256]{4,3,2,1,0:T(8,128)(2,1)}), bf16[32,8,2,16,256]{4,3,2,1,0:T(8,128)(2,1)}) %all-gather.4.cloned.1.call-update) | async-done | bytes 4194320 | tf_op jit(solution)/shard_map/all_gather | solution.py:294
  90.2 0.0 all-gather.6.cloned.1.call-update
  90.2 0.0 all-reduce.2.cloned.1.call-start
  90.3 0.0 copy-done.2
  90.3 0.1 add_select_fusion.3
  90.3 0.3 sine_multiply_fusion
  90.7 0.1 copy.30
  90.9 0.2 fusion.12
  91.0 0.0 copy-done.3
  91.0 0.4 multiply_convert_fusion
  91.4 0.3 copy.33
  91.7 0.0 copy-start
  91.7 1.3 copy.31.first_ref
  93.1 2.2 select_convert_fusion
  95.3 2.7 convert_element_type.51.second_ref
  98.0 0.0 copy-done
  98.0 0.6 gather_fusion
  98.7 0.6 pad_add_fusion.who_ref
  99.3 0.2 select_reduce_fusion
  99.5 0.6 add_select_fusion.1
  100.1 38.2 %shard_map.95.inter_ref = bf16[32,256,1024]{2,1,0:T(8,128)(2,1)} custom-call(bf16[64,32]{1,0:T(8,128)(2,1)} %constant.171.clone.line_ref, bf16[512,512]{1,0:T(8,128)(2,1)} %constant.172.clone.plane_ref, s32[16,1,512]{2,1,0:T(1,128)} %bitcast.30, bf16[512,8192]{1,0:T(8,128)(2,1)} %w_ref.1), custom_call_target="tpu_custom_call" | custom-call | flops 17179869184 | bytes 25165824 | tf_op jit(solution)/shard_map/pallas_call | solution.py:98
  138.4 0.0 all-gather.6.cloned.1.call-done
  138.4 66.6 %shard_map.96 = f32[8,2,64,64]{3,2,1,0:T(8,128)} custom-call(s32[17]{0:T(128)} %pad_add_fusion.who_ref, bf16[2,32,8,2,16,256]{5,4,3,2,1,0:T(8,128)(2,1)} %bitcast.31, bf16[32,256,1024]{2,1,0:T(8,128)(2,1)} %shard_map.95.inter_ref, bf16[2048,256]{1,0:T(8,128)(2,1)} %copy.31.first_ref, bf16[4,256,1024]{2,1,0:T(8,128)(2,1)} %convert_element_type.51.second_ref), custom_call_target="tpu_custom_call" | custom-call | flops 17179869184 | bytes 16777216 | tf_op jit(solution)/shard_map/pallas_call | solution.py:245
  205.0 2.0 reshape.498
  207.0 0.0 all-reduce.2.cloned.1.call-update
  207.1 105.5 %all-reduce.2.cloned.1.call-done = f32[8,2,4096]{2,1,0:T(2,128)} async-done(((f32[8,2,4096]{2,1,0:T(2,128)}), f32[8,2,4096]{2,1,0:T(2,128)}) %all-reduce.2.cloned.1.call-update) | async-done | bytes 262160 | tf_op jit(solution)/shard_map/psum | solution.py:300
  312.6 2.4 all_gather.15
  315.0 0.8 gather_fusion.1
  315.8 3.9 %gather.11 = f32[8,2,8,8,8,8]{5,4,3,2,1,0:T(8,128)} reshape(f32[8,2,4096]{2,1,0:T(2,128)S(1)} %gather_fusion.1) | data formatting | bytes 524288 | tf_op jit(solution)/shard_map/jit(_take)/gather | solution.py:310
  319.7 5.1 %select_bitcast_fusion = f32[8,2,8,8,8,8]{4,5,2,3,1,0:T(8,128)} fusion(f32[8,2,8,8,8,8]{5,4,3,2,1,0:T(8,128)} %gather.11, pred[8]{0:T(512)(128)(4,1)S(1)} %compare_and_fusion), kind=kLoop, calls=%fused_computation.2 | loop fusion | flops 65536 | bytes 524296 | tf_op jit(solution)/shard_map/transpose | solution.py:282
  324.8 5.4 %copy.32 = f32[8,2,8,8,8,8]{5,4,3,2,1,0:T(8,128)} copy(f32[8,2,8,8,8,8]{4,5,2,3,1,0:T(8,128)} %select_bitcast_fusion) | data formatting | bytes 524288 | tf_op jit(solution)/shard_map/transpose | solution.py:282
  330.2 0.0 copy-start.4
  330.2 0.0 copy-start.1
  330.2 3.8 %reshape.499 = f32[8,2,4096]{2,1,0:T(2,128)S(1)} reshape(f32[8,2,8,8,8,8]{5,4,3,2,1,0:T(8,128)} %copy.32) | data formatting | bytes 524288 | tf_op jit(solution)/shard_map/reshape | solution.py:283
  333.9 0.0 copy-done.4
  333.9 0.9 broadcast_multiply_fusion
  334.8 0.0 copy-done.1
  334.8 0.7 copy.37
  (14 shorter events, 0.1 us)
Async XLA Ops:
  7.2 83.9 %copy-start.3 = (f32[8,8]{0,1:T(8,128)S(1)}, f32[8,8]{0,1:T(8,128)}, u32[]{:S(2)}) copy-start(f32[8,8]{0,1:T(8,128)} %constant.173.clone) | copy-start | bytes 772
  7.2 83.1 %copy-start.2 = (s32[8192]{0:T(1024)S(1)}, s32[8192]{0:T(1024)}, u32[]{:S(2)}) copy-start(s32[8192]{0:T(1024)} %param.10) | copy-start | bytes 98308
  7.2 83.0 %all-gather.4.cloned.1.call-start = ((), (), s32[]{:S(2)}) async-start(), calls=%async_computation | async-start | bytes 4456448 | tf_op jit(solution)/shard_map/all_gather | solution.py:294
  8.9 129.4 %all-gather.6.cloned.1.call-start = ((), (), s32[]{:S(2)}) async-start(), calls=%async_computation.2 | async-start | bytes 12582912 | tf_op jit(solution)/shard_map/all_gather | solution.py:295
  90.2 222.4 %all-reduce.2.cloned.1.call-start = ((), (), s32[]{:S(2)}) async-start(), calls=%async_computation.1 | async-start | bytes 524288 | tf_op jit(solution)/shard_map/psum | solution.py:300
  91.7 6.3 %copy-start = (s32[16]{0:T(128)S(1)}, s32[16]{0:T(128)}, u32[]{:S(2)}) copy-start(s32[16]{0:T(128)} %param.9) | copy-start | bytes 196
  330.2 3.8 %copy-start.4 = (f32[2]{0:T(128)S(1)}, f32[2]{0:T(128)}, u32[]{:S(2)}) copy-start(f32[2]{0:T(128)} %constant.174.clone) | copy-start | bytes 28
  330.2 4.7 %copy-start.1 = (f32[8,2,4096]{2,1,0:T(2,128)S(1)}, f32[8,2,4096]{2,1,0:T(2,128)}, u32[]{:S(2)}) copy-start(f32[8,2,4096]{2,1,0:T(2,128)} %all-reduce.2.cloned.1.call-done) | copy-start | bytes 786436
Sparse Core Ops, SparseCore 0:
  11.4 78.7 all-gather.3
  91.7 18.4 all-gather.5
  207.2 105.3 all-reduce.1
where the time goes:
time: 343 us; the launch traced here: 342 us
  waiting for transfers between devices  187 us (55%)
  Pallas kernels  105 us (31%)
  local copies, waits for them, and re-layouts  23.4 us (7%)
  between operations  13.9 us (4%)
  other arithmetic  10.6 us (3%)
    psum x1, waiting for transfers between devices, on_device(): summed = lax.psum(part.reshape(pairs, 2, NC * NC * NV * NV), 'ga')  106 us
    all_gather x1, waiting for transfers between devices, on_device(): lax.all_gather(wavefunctions.transpose(3, 0, 1, 2, 4), 'ga', axis=0, tile...  81.2 us
    pallas_call x1, Pallas kernels, partial_kernel(): pl.pallas_call(functools.partial(contraction_kernel, pairs), grid_spec=sp...  66.6 us
    pallas_call x1, Pallas kernels, transformed_interaction(): pl.pallas_call(functools.partial(interaction_kernel, steps), grid=(steps...  38.2 us
  transfers between devices with their start and end apart: 3, of which 2 were waited for; matrix products, arithmetic and copies ran while one was open for 3% of the time, Pallas kernels for 11%

commit v1 on v0

--- a/solution.py
+++ b/solution.py
@@ -131,55 +131,62 @@
     )
 
 
-def contraction_kernel(
+def fill_planes(who_ref, waves_ref, pairs, store):
+    def fill(k, carry):
+        for z in range(STEP_Z):
+            home = waves_ref[who_ref[0], z, k].astype(F32)
+            away = waves_ref[who_ref[1 + k], z, who_ref[1 + pairs + k]].astype(F32)
+            real_part, imag_part = pair_rows((home[:8], home[8:]), (away[:8], away[8:]))
+            lanes = slice(z * NXY, (z + 1) * NXY)
+            start = pl.multiple_of(k * PAIRS, PAIRS)
+            store(pl.ds(start, PAIRS), lanes, real_part)
+            store(pl.ds(pairs * PAIRS + start, PAIRS), lanes, imag_part)
+        return carry
+
+    lax.fori_loop(0, pairs, fill, 0)
+
+
+def response_kernel(pairs, who_ref, waves_ref, inter_ref, out_ref, val_ref):
+    def store(rows, lanes, values):
+        val_ref[rows, lanes] = values.astype(BF)
+
+    fill_planes(who_ref, waves_ref, pairs, store)
+
+    @pl.when(pl.program_id(0) == 0)
+    def _():
+        out_ref[...] = jnp.zeros_like(out_ref)
+
+    inter = inter_ref[...].reshape(STEP_Z * NXY, inter_ref.shape[2])
+    out_ref[...] += jnp.dot(val_ref[...], inter, preferred_element_type=F32)
+
+
+def block_kernel(
     pairs,
     who_ref,
     waves_ref,
-    inter_ref,
+    response_ref,
     first_ref,
     second_ref,
     out_ref,
-    val_ref,
     cond_ref,
     cond_low_ref,
-    response_ref,
     spectrum_ref,
 ):
     step = pl.program_id(0)
     half = pairs * PAIRS
     rows = response_ref.shape[1] // 2
 
-    def fill(k, carry):
-        for z in range(STEP_Z):
-            home = waves_ref[who_ref[0], z, k].astype(F32)
-            away = waves_ref[who_ref[1 + k], z, who_ref[1 + pairs + k]].astype(F32)
-            for first in (0, NV):
-                left = (home[0, first : first + 8], home[1, first : first + 8])
-                right = (away[0, first : first + 8], away[1, first : first + 8])
-                real_part, imag_part = pair_rows(left, right)
-                start = pl.multiple_of(k * PAIRS, PAIRS)
-                lanes = slice(z * NXY, (z + 1) * NXY)
-                if first == 0:
-                    val_ref[pl.ds(start, PAIRS), lanes] = real_part.astype(BF)
-                    val_ref[pl.ds(half + start, PAIRS), lanes] = imag_part.astype(BF)
-                else:
-                    high, low = split(real_part)
-                    cond_ref[pl.ds(start, PAIRS), lanes] = high
-                    cond_low_ref[pl.ds(start, PAIRS), lanes] = low
-                    high, low = split(imag_part)
-                    cond_ref[pl.ds(half + start, PAIRS), lanes] = high
-                    cond_low_ref[pl.ds(half + start, PAIRS), lanes] = low
-        return carry
-
-    lax.fori_loop(0, pairs, fill, 0)
+    def store(where, lanes, values):
+        high, low = split(values)
+        cond_ref[where, lanes] = high
+        cond_low_ref[where, lanes] = low
+
+    fill_planes(who_ref, waves_ref, pairs, store)
 
     @pl.when(step == 0)
     def _():
-        response_ref[...] = jnp.zeros_like(response_ref)
         spectrum_ref[...] = jnp.zeros_like(spectrum_ref)
 
-    inter = inter_ref[...].reshape(STEP_Z * NXY, 2 * rows)
-    response_ref[...] += jnp.dot(val_ref[...], inter, preferred_element_type=F32)
     mixed = jnp.dot(cond_ref[...], first_ref[...], preferred_element_type=F32)
     mixed = mixed + jnp.dot(cond_low_ref[...], first_ref[...], preferred_element_type=F32)
     mixed, mixed_low = split(mixed)
@@ -210,47 +217,202 @@
             product = product + mixed_product(cond_low, resp) + mixed_product(cond, resp_low)
             scale = 1.0 / (NG * (SCALE_16 * SCALE_32) ** 2)
             a, b = product[:PAIRS], product[PAIRS:]
-            out_ref[k, 0] = (a[:, :PAIRS] + b[:, PAIRS:]) * scale
-            out_ref[k, 1] = (a[:, PAIRS:] - b[:, :PAIRS]) * scale
+            real_part = a[:, :PAIRS] + b[:, PAIRS:]
+            imag_part = a[:, PAIRS:] - b[:, :PAIRS]
+            out_ref[top, :] = jnp.concatenate([real_part, imag_part], axis=1) * scale
             return carry
 
         lax.fori_loop(0, pairs, finish, 0)
 
 
-def partial_kernel(who, waves, inter, first, second):
-    holders, _, pairs = waves.shape[:3]
+def waves_spec(waves):
+    shape = (waves.shape[0], STEP_Z) + waves.shape[2:]
+    return pl.BlockSpec(shape, lambda i, who: (0, i, 0, 0, 0))
+
+
+def all_responses(who, waves, inter):
+    pairs = waves.shape[2]
     rows2 = inter.shape[2]
     half2 = 2 * pairs * PAIRS
-    steps = NZ // STEP_Z
     spec = pltpu.PrefetchScalarGridSpec(
         num_scalar_prefetch=1,
-        grid=(steps,),
+        grid=(NZ // STEP_Z,),
         in_specs=[
-            pl.BlockSpec(
-                (holders, STEP_Z, pairs, 2, NV + NC, NXY), lambda i, who: (0, i, 0, 0, 0, 0)
-            ),
+            waves_spec(waves),
             pl.BlockSpec((STEP_Z, NXY, rows2), lambda i, who: (i, 0, 0)),
+        ],
+        out_specs=pl.BlockSpec((half2, rows2), lambda i, who: (0, 0)),
+        scratch_shapes=[pltpu.VMEM((half2, STEP_Z * NXY), BF)],
+    )
+    return pl.pallas_call(
+        functools.partial(response_kernel, pairs),
+        grid_spec=spec,
+        out_shape=jax.ShapeDtypeStruct((half2, rows2), F32),
+        compiler_params=pltpu.CompilerParams(vmem_limit_bytes=VMEM_LIMIT),
+        cost_estimate=pl.CostEstimate(
+            flops=2 * half2 * rows2 * NG, bytes_accessed=2 * inter.size, transcendentals=0
+        ),
+    )(who, waves, inter)
+
+
+def partial_blocks(who, waves, response, first, second):
+    pairs = waves.shape[2]
+    half2, rows2 = response.shape
+    spec = pltpu.PrefetchScalarGridSpec(
+        num_scalar_prefetch=1,
+        grid=(NZ // STEP_Z,),
+        in_specs=[
+            waves_spec(waves),
+            pl.BlockSpec((half2, rows2), lambda i, who: (0, 0)),
             pl.BlockSpec(first.shape, lambda i, who: (0, 0)),
             pl.BlockSpec((1,) + second.shape[1:], lambda i, who: (i, 0, 0)),
         ],
-        out_specs=pl.BlockSpec((pairs, 2, PAIRS, PAIRS), lambda i, who: (0, 0, 0, 0)),
+        out_specs=pl.BlockSpec((pairs * PAIRS, 2 * PAIRS), lambda i, who: (0, 0)),
         scratch_shapes=[
             pltpu.VMEM((half2, STEP_Z * NXY), BF),
             pltpu.VMEM((half2, STEP_Z * NXY), BF),
-            pltpu.VMEM((half2, STEP_Z * NXY), BF),
-            pltpu.VMEM((half2, rows2), F32),
             pltpu.VMEM((half2, rows2), F32),
         ],
     )
     return pl.pallas_call(
-        functools.partial(contraction_kernel, pairs),
+        functools.partial(block_kernel, pairs),
         grid_spec=spec,
-        out_shape=jax.ShapeDtypeStruct((pairs, 2, PAIRS, PAIRS), F32),
+        out_shape=jax.ShapeDtypeStruct((pairs * PAIRS, 2 * PAIRS), F32),
         compiler_params=pltpu.CompilerParams(vmem_limit_bytes=VMEM_LIMIT),
         cost_estimate=pl.CostEstimate(
-            flops=2 * half2 * rows2 * NG, bytes_accessed=2 * inter.size, transcendentals=0
-        ),
-    )(who, waves, inter, first, second)
+            flops=half2 * rows2 * NG, bytes_accessed=4 * response.size, transcendentals=0
+        ),
+    )(who, waves, response, first, second)
+
+
+def sum_kernel(
+    holders, members, part_ref, out_ref, got_ref, all_ref, send1, recv1, send2, recv2, send3, recv3
+):
+    ka = lax.axis_index("ka")
+    ga = lax.axis_index("ga")
+    size = part_ref.shape[0] // members
+    mesh_id = pl.DeviceIdType.MESH
+    barrier = pltpu.get_barrier_semaphore()
+
+    def member(d):
+        return lax.rem(ga + d, members)
+
+    def holder(e):
+        return lax.rem(ka + e, holders)
+
+    def block(place):
+        return pl.ds(pl.multiple_of(place * size, size), size)
+
+    def scatter(d):
+        return pltpu.make_async_remote_copy(
+            src_ref=part_ref.at[block(member(d))],
+            dst_ref=got_ref.at[d],
+            send_sem=send1.at[d],
+            recv_sem=recv1.at[d],
+            device_id=(ka, member(d)),
+            device_id_type=mesh_id,
+        )
+
+    def gather(d):
+        return pltpu.make_async_remote_copy(
+            src_ref=all_ref.at[ka, block(ga)],
+            dst_ref=all_ref.at[ka, block(ga)],
+            send_sem=send2.at[d],
+            recv_sem=recv2.at[d],
+            device_id=(ka, member(d)),
+            device_id_type=mesh_id,
+        )
+
+    def exchange(e):
+        return pltpu.make_async_remote_copy(
+            src_ref=all_ref.at[ka],
+            dst_ref=all_ref.at[ka],
+            send_sem=send3.at[e],
+            recv_sem=recv3.at[e],
+            device_id=(holder(e), ga),
+            device_id_type=mesh_id,
+        )
+
+    def loop(count, body):
+        def run(i, carry):
+            body(i)
+            return carry
+
+        lax.fori_loop(1, count, run, 0)
+
+    def greet(device):
+        pl.semaphore_signal(barrier, inc=1, device_id=device, device_id_type=mesh_id)
+
+    loop(members, lambda d: greet((ka, member(d))))
+    loop(holders, lambda e: greet((holder(e), ga)))
+    pl.semaphore_wait(barrier, members + holders - 2)
+
+    loop(members, lambda d: scatter(d).start())
+    all_ref[ka, block(ga), :] = part_ref[block(ga), :]
+
+    def add(d):
+        scatter(d).wait_recv()
+        all_ref[ka, block(ga), :] += got_ref[d]
+
+    loop(members, add)
+    loop(members, lambda d: gather(d).start())
+    loop(members, lambda d: gather(d).wait_recv())
+    loop(holders, lambda e: exchange(e).start())
+    loop(members, lambda d: scatter(d).wait_send())
+    loop(members, lambda d: gather(d).wait_send())
+    loop(holders, lambda e: exchange(e).wait())
+    out_ref[...] = all_ref[...]
+
+
+def summed_everywhere(part, holders, members):
+    rows, lanes = part.shape
+    size = rows // members
+    return pl.pallas_call(
+        functools.partial(sum_kernel, holders, members),
+        out_shape=jax.ShapeDtypeStruct((holders, rows, lanes), F32),
+        in_specs=[pl.BlockSpec(memory_space=pltpu.VMEM)],
+        out_specs=pl.BlockSpec(memory_space=pltpu.VMEM),
+        scratch_shapes=[
+            pltpu.VMEM((members, size, lanes), F32),
+            pltpu.VMEM((holders, rows, lanes), F32),
+        ]
+        + [pltpu.SemaphoreType.DMA((members,))] * 4
+        + [pltpu.SemaphoreType.DMA((holders,))] * 2,
+        compiler_params=pltpu.CompilerParams(
+            collective_id=0, has_side_effects=True, vmem_limit_bytes=VMEM_LIMIT
+        ),
+    )(part)
+
+
+def mirror_kernel(source_ref, blocks_ref, out_ref):
+    del source_ref
+
+    def swapped(size, axis):
+        row = lax.broadcasted_iota(jnp.int32, (size, size), axis)
+        column = lax.broadcasted_iota(jnp.int32, (size, size), 1 - axis)
+        inner = row % PAIRS
+        return (column == row - inner + (inner % 8) * 8 + inner // 8).astype(F32)
+
+    highest = lax.Precision.HIGHEST
+    left = jnp.dot(swapped(PAIRS, 0), blocks_ref[0], precision=highest)
+    both = jnp.dot(left, swapped(2 * PAIRS, 1), precision=highest)
+    lane = lax.broadcasted_iota(jnp.int32, both.shape, 1)
+    out_ref[0] = jnp.where(lane < PAIRS, both, -both)
+
+
+def mirrored(source, blocks):
+    shape = (1,) + blocks.shape[1:]
+    spec = pltpu.PrefetchScalarGridSpec(
+        num_scalar_prefetch=1,
+        grid=(source.shape[0],),
+        in_specs=[pl.BlockSpec(shape, lambda i, source: (source[i], 0, 0))],
+        out_specs=pl.BlockSpec(shape, lambda i, source: (i, 0, 0)),
+    )
+    return pl.pallas_call(
+        mirror_kernel,
+        grid_spec=spec,
+        out_shape=jax.ShapeDtypeStruct((source.shape[0],) + blocks.shape[1:], F32),
+    )(source, blocks)
 
 
 def local_tables(gmap, place, rows):
@@ -275,30 +437,34 @@
     return first, second
 
 
-def swap_blocks(blocks):
+def flattened(blocks):
     number = blocks.shape[0]
-    moved = (
-        blocks.reshape(number, 2, NC, NC, NV, NV)
-        .transpose(0, 1, 3, 2, 5, 4)
-        .reshape(number, 2, NC * NC * NV * NV)
-    )
-    return moved * jnp.array([1.0, -1.0], dtype=F32)[None, :, None]
-
-
-def on_device(wavefunctions, partner, gmap, screened):
-    pairs = wavefunctions.shape[0]
+    parts = blocks.reshape(number, PAIRS, 2, PAIRS).transpose(0, 2, 1, 3)
+    return parts.reshape(number, 2, PAIRS * PAIRS)
+
+
+def on_device(holders, members, wavefunctions, partner, gmap, screened):
+    pairs, _, _, planes, _ = wavefunctions.shape
     ka_place = lax.axis_index("ka")
     ga_place = lax.axis_index("ga")
     owned = ka_place * pairs + jnp.arange(pairs, dtype=jnp.int32)
     wanted = partner[owned]
-    waves = lax.all_gather(wavefunctions.transpose(3, 0, 1, 2, 4), "ga", axis=0, tiled=True)
-    waves = lax.all_gather(waves, "ka", axis=0)
+    by_plane = wavefunctions.transpose(3, 0, 1, 2, 4)
+    val = by_plane[:, :, :, :NV].reshape(planes, pairs, 2 * NV, NXY)
+    cond = by_plane[:, :, :, NV:].reshape(planes, pairs, 2 * NC, NXY)
+    val = lax.all_gather(val, "ga", axis=0, tiled=True)
     inter = transformed_interaction(gmap, screened)
     first, second = local_tables(gmap, ga_place, screened.shape[0])
+    val, cond, inter, first, second = lax.optimization_barrier((val, cond, inter, first, second))
+    val = lax.all_gather(val, "ka", axis=0)
+    cond = lax.all_gather(cond, "ga", axis=0, tiled=True)
     who = jnp.concatenate([ka_place[None].astype(jnp.int32), wanted // pairs, wanted % pairs])
-    part = partial_kernel(who, waves, inter, first, second)
-    summed = lax.psum(part.reshape(pairs, 2, NC * NC * NV * NV), "ga")
-    everyone = lax.all_gather(summed, "ka", axis=0, tiled=True)
+    response = all_responses(who, val, inter)
+    cond, response = lax.optimization_barrier((cond, response))
+    cond = lax.all_gather(cond, "ka", axis=0)
+    part = partial_blocks(who, cond, response, first, second)
+    everyone = summed_everywhere(part, holders, members)
+    everyone = everyone.reshape(holders * pairs, PAIRS, 2 * PAIRS)
     source = jnp.sum(
         jnp.where(
             partner[None, :] == owned[:, None],
@@ -307,13 +473,17 @@
         ),
         axis=1,
     )
-    mirror_out = swap_blocks(jnp.take(everyone, source, axis=0))
-    return (summed, mirror_out)
+    own = lax.dynamic_slice_in_dim(everyone, ka_place * pairs, pairs)
+    return (flattened(own), flattened(mirrored(source, everyone)))
 
 
 def solution(mesh):
     in_specs = (P("ka", None, None, "ga", None), P(), P(), P("ga", None))
     out_specs = (P("ka", None, None), P("ka", None, None))
     return jax.shard_map(
-        on_device, mesh=mesh, in_specs=in_specs, out_specs=out_specs, check_vma=False
-    )
+        functools.partial(on_device, mesh.shape["ka"], mesh.shape["ga"]),
+        mesh=mesh,
+        in_specs=in_specs,
+        out_specs=out_specs,
+        check_vma=False,
+    )

time: 343 us -> 249 us (0.73)
  waiting for transfers between devices: 187 us -> 78 us
  Pallas kernels: 105 us -> 138 us
  local copies, waits for them, and re-layouts: 23.4 us -> 11.3 us
  other arithmetic: 10.6 us -> 5.89 us
    psum x1 -> x0, waiting for transfers between devices: 106 us -> none  [on_device(): summed = lax.psum(part.reshape(pairs, 2, NC * NC * NV * NV), 'ga')]
    pallas_call x1 -> x4, Pallas kernels: 66.6 us -> 101 us  [the longest x1 41 us: partial_blocks(): pl.pallas_call(functools.partial(block_kernel, pairs), grid_spec=spec, ou...]
    transpose x1, local copies, waits for them, and re-layouts: 5.35 us -> 0.04 us  [flattened(): parts = blocks.reshape(number, PAIRS, 2, PAIRS).transpose(0, 2, 1, 3)]
    transpose x1 -> x0, other arithmetic: 5.07 us -> none  [swap_blocks(): moved = blocks.reshape(number, 2, NC, NC, NV, NV).transpose(0, 1, 3, 2, 5...]
    gather x2 -> x0, local copies, waits for them, and re-layouts: 4.76 us -> none  [on_device(): mirror_out = swap_blocks(jnp.take(everyone, source, axis=0))]
    all_gather x2 -> x4, waiting for transfers between devices: 81.2 us -> 77.3 us  [the longest x1 34.6 us: on_device(): cond = lax.all_gather(cond, 'ga', axis=0, tiled=True)]
  transfers between devices with their start and end apart: 3 -> 4, of which waited for: 2 -> 4; matrix products, arithmetic and copies ran while one was open for 3% -> 5% of each run, Pallas kernels for 11% -> 28%
where the time goes in v1:
time: 249 us; the launch traced here: 248 us
  Pallas kernels  138 us (55%)
  waiting for transfers between devices  78 us (31%)
  between operations  14 us (6%)
  local copies, waits for them, and re-layouts  11.3 us (5%)
  other arithmetic  5.89 us (2%)
    pallas_call x1, Pallas kernels, partial_blocks(): pl.pallas_call(functools.partial(block_kernel, pairs), grid_spec=spec, ou...  41 us
    pallas_call x1, Pallas kernels, transformed_interaction(): pl.pallas_call(functools.partial(interaction_kernel, steps), grid=(steps...  37.7 us
    all_gather x1, waiting for transfers between devices, on_device(): cond = lax.all_gather(cond, 'ga', axis=0, tiled=True)  34.6 us
    pallas_call x1, Pallas kernels, all_responses(): pl.pallas_call(functools.partial(response_kernel, pairs), grid_spec=spec,...  30.7 us
    pallas_call x1, Pallas kernels, summed_everywhere(): pl.pallas_call(functools.partial(sum_kernel, holders, members), out_shape...  22.4 us
    all_gather x1, waiting for transfers between devices, on_device(): val = lax.all_gather(val, 'ga', axis=0, tiled=True)  19.4 us
    all_gather x1, waiting for transfers between devices, on_device(): cond = lax.all_gather(cond, 'ka', axis=0)  11.7 us
    all_gather x1, waiting for transfers between devices, on_device(): val = lax.all_gather(val, 'ka', axis=0)  11.5 us
  transfers between devices with their start and end apart: 4, of which 4 were waited for; matrix products, arithmetic and copies ran while one was open for 5% of the time, Pallas kernels for 28%

profile of v1, /device:TPU:0, one launch (start us, length us, event | category | flops | bytes accessed | tf_op | source)
XLA Modules:
  0.0 247.9 jit_solution(9487131686596106309)
XLA Ops:
  7.2 0.0 all-gather.7.cloned.1.call-start
  7.2 1.2 fusion.20
  8.4 0.7 copy.52
  9.0 0.0 all-gather.7.cloned.1.call-update
  9.1 0.0 all-gather.11.cloned.1.call-start
  9.1 0.8 add_select_fusion.3
  9.9 0.3 sine_multiply_fusion
  10.2 0.1 copy.41
  10.4 2.2 select_convert_fusion
  12.6 0.0 copy-start.3
  12.7 2.8 %convert_element_type.53.second_ref = bf16[4,256,1024]{2,1,0:T(8,128)(2,1)} reshape(bf16[32,2,16,2,512]{4,3,2,1,0:T(2,128)(2,1)S(1)} %select_convert_fusion) | data formatting | bytes 4194304 | tf_op jit(solution)/shard_map/convert_element_type | solution.py:436
  15.5 0.0 copy-start.2
  15.5 0.2 fusion.12
  15.6 0.0 copy-done.3
  15.7 0.4 multiply_convert_fusion
  16.0 0.3 copy.48
  16.3 0.7 copy.51
  17.0 0.0 copy-done.2
  17.0 0.6 add_select_fusion.1
  17.6 37.7 %shard_map.86.inter_ref = bf16[32,256,1024]{2,1,0:T(8,128)(2,1)} custom-call(bf16[64,32]{1,0:T(8,128)(2,1)} %constant.156.clone.line_ref, bf16[512,512]{1,0:T(8,128)(2,1)} %constant.157.clone.plane_ref, s32[16,1,512]{2,1,0:T(1,128)} %bitcast.38, bf16[512,8192]{1,0:T(8,128)(2,1)} %w_ref.1), custom_call_target="tpu_custom_call" | custom-call | flops 17179869184 | bytes 25165824 | tf_op jit(solution)/shard_map/pallas_call | solution.py:98
  55.4 0.0 copy-start
  55.4 19.4 %all-gather.7.cloned.1.call-done = bf16[32,8,16,256]{3,2,1,0:T(8,128)(2,1)} async-done(((bf16[2,8,16,256]{3,2,1,0:T(8,128)(2,1)}), bf16[32,8,16,256]{3,2,1,0:T(8,128)(2,1)}) %all-gather.7.cloned.1.call-update) | async-done | bytes 2097168 | tf_op jit(solution)/shard_map/all_gather | solution.py:455
  74.8 0.0 all-gather.11.cloned.1.call-update
  74.8 0.0 all-gather.9.cloned.1.call-start
  74.9 0.7 all-gather.9.cloned.1.call-update
  75.6 0.2 all-gather.13.cloned.1.call-start
  75.8 0.0 copy-done
  75.8 0.6 gather_fusion
  76.5 0.7 pad_add_fusion.who_ref
  77.2 11.5 %all-gather.11.cloned.1.call-done = bf16[64,8,16,256]{3,2,1,0:T(8,128)(2,1)} async-done(((bf16[32,8,16,256]{3,2,1,0:T(8,128)(2,1)}), bf16[64,8,16,256]{3,2,1,0:T(8,128)(2,1)}) %all-gather.11.cloned.1.call-update) | async-done | bytes 4194320 | tf_op jit(solution)/shard_map/all_gather | solution.py:459
  88.7 30.7 %shard_map.87.response_ref = f32[1024,1024]{1,0:T(8,128)} custom-call(s32[17]{0:T(128)} %pad_add_fusion.who_ref, bf16[2,32,8,16,256]{4,3,2,1,0:T(8,128)(2,1)} %bitcast.39, bf16[32,256,1024]{2,1,0:T(8,128)(2,1)} %shard_map.86.inter_ref), custom_call_target="tpu_custom_call" | custom-call | flops 17179869184 | bytes 16777216 | tf_op jit(solution)/shard_map/pallas_call | solution.py:247
  119.4 34.6 %all-gather.9.cloned.1.call-done = bf16[32,8,16,256]{3,2,1,0:T(8,128)(2,1)} async-done(((bf16[2,8,16,256]{3,2,1,0:T(8,128)(2,1)}), bf16[32,8,16,256]{3,2,1,0:T(8,128)(2,1)}) %all-gather.9.cloned.1.call-update) | async-done | bytes 2097168 | tf_op jit(solution)/shard_map/all_gather | solution.py:460
  153.9 0.0 all-gather.13.cloned.1.call-update
  154.0 0.7 select_reduce_fusion.source_ref
  154.7 1.3 copy.42.first_ref
  156.0 11.7 %all-gather.13.cloned.1.call-done = bf16[64,8,16,256]{3,2,1,0:T(8,128)(2,1)} async-done(((bf16[32,8,16,256]{3,2,1,0:T(8,128)(2,1)}), bf16[64,8,16,256]{3,2,1,0:T(8,128)(2,1)}) %all-gather.13.cloned.1.call-update) | async-done | bytes 4194320 | tf_op jit(solution)/shard_map/all_gather | solution.py:464
  167.7 41.0 %shard_map.88.part_ref = f32[512,128]{1,0:T(8,128)} custom-call(s32[17]{0:T(128)} %pad_add_fusion.who_ref, bf16[2,32,8,16,256]{4,3,2,1,0:T(8,128)(2,1)} %bitcast.40, f32[1024,1024]{1,0:T(8,128)} %shard_map.87.response_ref, bf16[2048,256]{1,0:T(8,128)(2,1)} %copy.42.first_ref, bf16[4,256,1024]{2,1,0:T(8,128)(2,1)} %convert_element_type.53.second_ref), custom_call_target="tpu_custom_call" | custom-call | flops 8589934592 | bytes 4194304 | tf_op jit(solution)/shard_map/pallas_call | solution.py:277
  208.7 22.4 %shard_map.89 = f32[2,512,128]{2,1,0:T(8,128)} custom-call(f32[512,128]{1,0:T(8,128)} %shard_map.88.part_ref), custom_call_target="tpu_custom_call" | custom-call | tf_op jit(solution)/shard_map/pallas_call | solution.py:370
  231.1 0.0 copy-start.1
  231.1 6.6 %shard_map.90 = f32[8,64,128]{2,1,0:T(8,128)} custom-call(s32[8]{0:T(128)} %select_reduce_fusion.source_ref, f32[16,64,128]{2,1,0:T(8,128)} %bitcast.31), custom_call_target="tpu_custom_call" | custom-call | tf_op jit(solution)/shard_map/pallas_call | solution.py:411
  237.7 1.3 reshape.497
  239.0 1.0 reshape.498
  240.0 0.0 copy-done.1
  240.0 0.3 reshape.495
  240.4 1.0 reshape.509
  (14 shorter events, 0.2 us)
Async XLA Ops:
  7.2 67.6 %all-gather.7.cloned.1.call-start = ((), (), s32[]{:S(2)}) async-start(), calls=%async_computation | async-start | bytes 2228224 | tf_op jit(solution)/shard_map/all_gather | solution.py:455
  9.1 79.6 %all-gather.11.cloned.1.call-start = ((), (), s32[]{:S(2)}) async-start(), calls=%async_computation.2 | async-start | bytes 6291456 | tf_op jit(solution)/shard_map/all_gather | solution.py:459
  12.6 3.0 %copy-start.3 = (f32[8,8]{0,1:T(8,128)S(1)}, f32[8,8]{0,1:T(8,128)}, u32[]{:S(2)}) copy-start(f32[8,8]{0,1:T(8,128)} %constant.158.clone) | copy-start | bytes 772
  15.5 1.6 copy-start.2
  55.4 20.4 %copy-start = (s32[16]{0:T(128)S(1)}, s32[16]{0:T(128)}, u32[]{:S(2)}) copy-start(s32[16]{0:T(128)} %param.8) | copy-start | bytes 196
  74.8 79.1 %all-gather.9.cloned.1.call-start = ((), (), s32[]{:S(2)}) async-start(), calls=%async_computation.1 | async-start | bytes 2228224 | tf_op jit(solution)/shard_map/all_gather | solution.py:460
  75.6 92.1 %all-gather.13.cloned.1.call-start = ((), (), s32[]{:S(2)}) async-start(), calls=%async_computation.3 | async-start | bytes 6291456 | tf_op jit(solution)/shard_map/all_gather | solution.py:464
  231.1 8.9 %copy-start.1 = (f32[2,512,128]{2,1,0:T(8,128)S(1)}, f32[2,512,128]{2,1,0:T(8,128)}, u32[]{:S(2)}) copy-start(f32[2,512,128]{2,1,0:T(8,128)} %shard_map.89) | copy-start | bytes 1572868
Sparse Core Ops, SparseCore 0:
  11.3 63.4 all-gather.6
  76.3 12.3 all-gather.10
  92.0 61.8 all-gather.8
  155.3 12.3 all-gather.12

commit v2 on v1

--- a/solution.py
+++ b/solution.py
@@ -18,6 +18,8 @@
 NG = NXY * NZ
 PAIRS = 64
 GROUP = 256
+SECOND_STAGE = 17
+THIRD_STAGE = 25
 STEP_Z = 8
 BF = jnp.bfloat16
 F32 = jnp.float32
@@ -45,11 +47,130 @@
     return SCALE_16 * np.block([[c, -s], [s, c]])
 
 
-def interaction_kernel(steps, line_ref, plane_ref, gz_ref, w_ref, out_ref, mid_ref, low_ref):
+def gather_stages(holders, members, shards, wholes, sems):
+    far, near, across, own = sems
+    ka = lax.axis_index("ka")
+    ga = lax.axis_index("ga")
+    firsts = members // 4
+    first, quad = ga // 4, ga % 4
+    by_one = quad + 1 - 2 * (quad % 2)
+    by_two = (quad + 2) % 4
+    by_both = (by_one + 2) % 4
+    mesh_id = pl.DeviceIdType.MESH
+    barrier = pltpu.get_barrier_semaphore()
+    orders = ((by_one, by_two), (by_two, by_one))
+
+    def remote(src, dst, send, recv, device):
+        return pltpu.make_async_remote_copy(
+            src_ref=src,
+            dst_ref=dst,
+            send_sem=send,
+            recv_sem=recv,
+            device_id=device,
+            device_id_type=mesh_id,
+        )
+
+    def over_first(h, d):
+        target = ((first + d) % firsts) * 4 + quad
+        dst = wholes[h].at[ka, first, quad]
+        return remote(shards[h], dst, far.at[0, h, d], far.at[1, h, d], (ka, target))
+
+    def in_quad(h, index):
+        place = (quad, quad, orders[h][0])[index]
+        target = first * 4 + orders[h][0 if index == 0 else 1]
+        block = wholes[h].at[ka, :, place]
+        return remote(block, block, near.at[0, h, index], near.at[1, h, index], (ka, target))
+
+    def to_holder(h, index, e):
+        place = (quad, orders[h][0], orders[h][1], by_both)[index]
+        block = wholes[h].at[ka, :, place]
+        device = ((ka + e) % holders, ga)
+        return remote(block, block, across.at[0, h, index, e], across.at[1, h, index, e], device)
+
+    def place_own(h):
+        return pltpu.make_async_copy(shards[h], wholes[h].at[ka, first, quad], own.at[h])
+
+    def greet(device):
+        pl.semaphore_signal(barrier, inc=1, device_id=device, device_id_type=mesh_id)
+
+    distances = range(1, firsts)
+    others = range(1, holders)
+
+    def enter():
+        for d in distances:
+            greet((ka, ((first + d) % firsts) * 4 + quad))
+        for place in (by_one, by_two):
+            greet((ka, first * 4 + place))
+        for e in others:
+            greet(((ka + e) % holders, ga))
+        pl.semaphore_wait(barrier, firsts - 1 + 2 + holders - 1)
+        for h in range(2):
+            for d in distances:
+                over_first(h, d).start()
+            place_own(h).start()
+
+    def second():
+        for h in range(2):
+            place_own(h).wait()
+            for d in distances:
+                over_first(h, d).wait_recv()
+            in_quad(h, 0).start()
+            for e in others:
+                to_holder(h, 0, e).start()
+
+    def third():
+        for h in range(2):
+            in_quad(h, 0).wait_recv()
+            in_quad(h, 1).start()
+            in_quad(h, 2).start()
+            for e in others:
+                to_holder(h, 1, e).start()
+
+    def leave():
+        for h in range(2):
+            for index in (1, 2):
+                in_quad(h, index).wait_recv()
+                for e in others:
+                    to_holder(h, index + 1, e).start()
+        for h in range(2):
+            for d in distances:
+                over_first(h, d).wait_send()
+            for index in range(3):
+                in_quad(h, index).wait_send()
+            for index in range(4):
+                for e in others:
+                    to_holder(h, index, e).wait()
+
+    return enter, second, third, leave
+
+
+def interaction_kernel(
+    steps,
+    holders,
+    members,
+    line_ref,
+    plane_ref,
+    gz_ref,
+    w_ref,
+    val_ref,
+    cond_ref,
+    out_ref,
+    all_val_ref,
+    all_cond_ref,
+    mid_ref,
+    low_ref,
+    *sems,
+):
     step = pl.program_id(0)
     rows = w_ref.shape[0]
     per = w_ref.shape[1] // GROUP
     cols = GROUP // NZ
+    enter, second, third, leave = gather_stages(
+        holders, members, (val_ref, cond_ref), (all_val_ref, all_cond_ref), sems
+    )
+    pl.when(step == 0)(enter)
+    pl.when(step == SECOND_STAGE)(second)
+    pl.when(step == THIRD_STAGE)(third)
 
     @pl.when(step < steps)
     def _():
@@ -87,33 +208,60 @@
             out_ref[i, :, :rows] = got[:NXY]
             out_ref[i, :, rows:] = got[NXY:]
 
-
-def transformed_interaction(gmap, screened):
+    pl.when(step == pl.num_programs(0) - 1)(leave)
+
+
+def transformed_interaction(holders, members, gmap, screened, val, cond):
     rows = screened.shape[0]
     per = 2
     steps = NG // (GROUP * per)
     planes = 2
     gz = (gmap % NZ).reshape(steps, 1, GROUP * per)
     last = steps - 1
-    return pl.pallas_call(
-        functools.partial(interaction_kernel, steps),
+    whole = jax.ShapeDtypeStruct((holders, members // 4, 4) + val.shape, BF)
+    dma = pltpu.SemaphoreType.DMA
+    anywhere = pl.BlockSpec(memory_space=pl.ANY)
+    inter, val, cond = pl.pallas_call(
+        functools.partial(interaction_kernel, steps, holders, members),
         grid=(steps + NZ // planes,),
         in_specs=[
             pl.BlockSpec((2 * NZ, NZ), lambda i: (0, 0)),
             pl.BlockSpec((2 * NXY, 2 * NXY), lambda i: (0, 0)),
             pl.BlockSpec((1, 1, GROUP * per), lambda i: (jnp.minimum(i, last), 0, 0)),
             pl.BlockSpec((rows, GROUP * per), lambda i: (0, jnp.minimum(i, last))),
+            anywhere,
+            anywhere,
         ],
-        out_specs=pl.BlockSpec(
-            (planes, NXY, 2 * rows), lambda i: (jnp.maximum(i - steps, 0), 0, 0)
+        out_specs=[
+            pl.BlockSpec((planes, NXY, 2 * rows), lambda i: (jnp.maximum(i - steps, 0), 0, 0)),
+            anywhere,
+            anywhere,
+        ],
+        out_shape=[jax.ShapeDtypeStruct((NZ, NXY, 2 * rows), BF), whole, whole],
+        scratch_shapes=[
+            pltpu.VMEM((NZ, 2, NXY, rows), BF),
+            pltpu.VMEM((NZ, 2, NXY, rows), BF),
+            dma((2, 2, members // 4)),
+            dma((2, 2, 3)),
+            dma((2, 2, 4, holders)),
+            dma((2,)),
+        ],
+        compiler_params=pltpu.CompilerParams(
+            collective_id=1, has_side_effects=True, vmem_limit_bytes=VMEM_LIMIT
         ),
-        out_shape=jax.ShapeDtypeStruct((NZ, NXY, 2 * rows), BF),
-        scratch_shapes=[pltpu.VMEM((NZ, 2, NXY, rows), BF)] * 2,
-        compiler_params=pltpu.CompilerParams(vmem_limit_bytes=VMEM_LIMIT),
         cost_estimate=pl.CostEstimate(
             flops=16 * NXY * NG * rows, bytes_accessed=6 * NG * rows, transcendentals=0
         ),
-    )(jnp.asarray(line_table(), BF), jnp.asarray(plane_table(), BF), gz, screened)
+    )(
+        jnp.asarray(line_table(), BF),
+        jnp.asarray(plane_table(), BF),
+        gz,
+        screened,
+        val,
+        cond,
+    )
+    shape = (holders, NZ) + val.shape[4:]
+    return inter, val.reshape(shape), cond.reshape(shape)
 
 
 def pair_rows(left, right):
@@ -452,16 +600,10 @@
     by_plane = wavefunctions.transpose(3, 0, 1, 2, 4)
     val = by_plane[:, :, :, :NV].reshape(planes, pairs, 2 * NV, NXY)
     cond = by_plane[:, :, :, NV:].reshape(planes, pairs, 2 * NC, NXY)
-    val = lax.all_gather(val, "ga", axis=0, tiled=True)
-    inter = transformed_interaction(gmap, screened)
+    inter, val, cond = transformed_interaction(holders, members, gmap, screened, val, cond)
     first, second = local_tables(gmap, ga_place, screened.shape[0])
-    val, cond, inter, first, second = lax.optimization_barrier((val, cond, inter, first, second))
-    val = lax.all_gather(val, "ka", axis=0)
-    cond = lax.all_gather(cond, "ga", axis=0, tiled=True)
     who = jnp.concatenate([ka_place[None].astype(jnp.int32), wanted // pairs, wanted % pairs])
     response = all_responses(who, val, inter)
-    cond, response = lax.optimization_barrier((cond, response))
-    cond = lax.all_gather(cond, "ka", axis=0)
     part = partial_blocks(who, cond, response, first, second)
     everyone = summed_everywhere(part, holders, members)
     everyone = everyone.reshape(holders * pairs, PAIRS, 2 * PAIRS)

time: 249 us -> 190 us (0.76)
  waiting for transfers between devices: 78 us -> 0 us
  Pallas kernels: 138 us -> 169 us
  between operations: 14 us -> 0.81 us
    all_gather x4 -> x0, waiting for transfers between devices: 77.3 us -> none  [the longest x1 34.6 us: on_device(): cond = lax.all_gather(cond, 'ga', axis=0, tiled=True)]
    pallas_call x1, Pallas kernels: 37.7 us -> 68 us  [transformed_interaction(): pl.pallas_call(functools.partial(interaction_kernel, steps, holders, memb...]
  transfers between devices with their start and end apart: 4 -> 0, of which waited for: 4 -> 0; matrix products, arithmetic and copies ran while one was open for 5% -> 0% of each run, Pallas kernels for 28% -> 0%
where the time goes in v2:
time: 190 us; the launch traced here: 189 us
  Pallas kernels  169 us (89%)
  local copies, waits for them, and re-layouts  12.3 us (6%)
  other arithmetic  6.62 us (3%)
    pallas_call x1, Pallas kernels, transformed_interaction(): pl.pallas_call(functools.partial(interaction_kernel, steps, holders, memb...  68 us
    pallas_call x1, Pallas kernels, partial_blocks(): pl.pallas_call(functools.partial(block_kernel, pairs), grid_spec=spec, ou...  41.2 us
    pallas_call x1, Pallas kernels, all_responses(): pl.pallas_call(functools.partial(response_kernel, pairs), grid_spec=spec,...  30.8 us
    pallas_call x1, Pallas kernels, summed_everywhere(): pl.pallas_call(functools.partial(sum_kernel, holders, members), out_shape...  22.6 us
    pallas_call x1, Pallas kernels, mirrored(): pl.pallas_call(mirror_kernel, grid_spec=spec, out_shape=jax.ShapeDtypeStr...  6.47 us

profile of v2, /device:TPU:0, one launch (start us, length us, event | category | flops | bytes accessed | tf_op | source)
XLA Modules:
  0.0 188.8 jit_solution(3483097102073555077)
XLA Ops:
  0.7 1.3 gather_fusion
  2.0 0.6 pad_add_fusion.who_ref
  2.6 1.4 add_select_fusion.1
  4.0 1.2 fusion.20
  5.1 0.7 copy_bitcast_fusion
  5.9 68.0 %shard_map.86 = (bf16[32,256,1024]{2,1,0:T(8,128)(2,1)}, bf16[2,4,4,2,8,16,256]{6,5,4,3,2,1,0:T(8,128)(2,1)}, bf16[2,4,4,2,8,16,256]{6,5,4,3,2,1,0:T(8,128)(2,1)}) custom-call(bf16[64,32]{1,0:T(8,128)(2,1)} %constant.156.clone.line_ref, bf16[512,512]{1,0:T(8,128)(2,1)} %constant.157.clone.plane_ref, s32[16,1,512]{2,1,0:T(1,128)} %bitcast.34, ...), custom_call_target="tpu_custom_call" | custom-call | flops 17179869184 | bytes 25165824 | tf_op jit(solution)/shard_map/pallas_call | solution.py:224
  73.8 0.0 copy-start.1
  73.8 30.8 %shard_map.87.response_ref = f32[1024,1024]{1,0:T(8,128)} custom-call(s32[17]{0:T(128)} %pad_add_fusion.who_ref, bf16[2,32,8,16,256]{4,3,2,1,0:T(8,128)(2,1)} %bitcast.36, bf16[32,256,1024]{2,1,0:T(8,128)(2,1)} %get-tuple-element.7.inter_ref), custom_call_target="tpu_custom_call" | custom-call | flops 17179869184 | bytes 16777216 | tf_op jit(solution)/shard_map/pallas_call | solution.py:395
  104.7 0.2 fusion.12
  104.9 0.0 copy-done.1
  104.9 0.4 multiply_convert_fusion
  105.2 0.3 copy.41
  105.6 1.3 copy.35.first_ref
  106.9 0.8 add_select_fusion.3
  107.7 0.3 sine_multiply_fusion
  108.0 0.1 copy.34
  108.1 2.2 %select_convert_fusion = bf16[32,2,16,2,512]{4,3,2,1,0:T(2,128)(2,1)S(1)} fusion(pred[16,512]{1,0:T(8,128)(4,1)S(1)} %iota_compare_fusion, bf16[32,2,2,512]{3,2,1,0:T(2,128)(2,1)S(1)} %copy.34), kind=kLoop, calls=%fused_computation.1 | loop fusion | flops 1048576 | bytes 2236416 | tf_op jit(solution)/shard_map/convert_element_type | solution.py:584
  110.4 2.7 %convert_element_type.51.second_ref = bf16[4,256,1024]{2,1,0:T(8,128)(2,1)} reshape(bf16[32,2,16,2,512]{4,3,2,1,0:T(2,128)(2,1)S(1)} %select_convert_fusion) | data formatting | bytes 4194304 | tf_op jit(solution)/shard_map/convert_element_type | solution.py:584
  113.1 41.2 %shard_map.88.part_ref = f32[512,128]{1,0:T(8,128)} custom-call(s32[17]{0:T(128)} %pad_add_fusion.who_ref, bf16[2,32,8,16,256]{4,3,2,1,0:T(8,128)(2,1)} %bitcast.35, f32[1024,1024]{1,0:T(8,128)} %shard_map.87.response_ref, bf16[2048,256]{1,0:T(8,128)(2,1)} %copy.35.first_ref, bf16[4,256,1024]{2,1,0:T(8,128)(2,1)} %convert_element_type.51.second_ref), custom_call_target="tpu_custom_call" | custom-call | flops 8589934592 | bytes 4194304 | tf_op jit(solution)/shard_map/pallas_call | solution.py:425
  154.3 0.0 copy-start
  154.3 22.6 %shard_map.89 = f32[2,512,128]{2,1,0:T(8,128)} custom-call(f32[512,128]{1,0:T(8,128)} %shard_map.88.part_ref), custom_call_target="tpu_custom_call" | custom-call | tf_op jit(solution)/shard_map/pallas_call | solution.py:518
  176.9 1.0 constant_dynamic-slice_fusion
  177.9 0.3 reshape.503
  178.3 1.0 reshape.515
  179.3 0.0 copy-done
  179.3 0.7 select_reduce_fusion.source_ref
  180.0 6.5 %shard_map.90 = f32[8,64,128]{2,1,0:T(8,128)} custom-call(s32[8]{0:T(128)} %select_reduce_fusion.source_ref, f32[16,64,128]{2,1,0:T(8,128)} %bitcast.30), custom_call_target="tpu_custom_call" | custom-call | tf_op jit(solution)/shard_map/pallas_call | solution.py:559
  186.5 1.3 reshape.505
  187.8 1.0 reshape.506
  (13 shorter events, 0.2 us)
Async XLA Ops:
  73.8 31.0 %copy-start.1 = (f32[8,8]{0,1:T(8,128)S(1)}, f32[8,8]{0,1:T(8,128)}, u32[]{:S(2)}) copy-start(f32[8,8]{0,1:T(8,128)} %constant.158.clone) | copy-start | bytes 772
  154.3 25.0 %copy-start = (s32[16]{0:T(128)S(1)}, s32[16]{0:T(128)}, u32[]{:S(2)}) copy-start(s32[16]{0:T(128)} %param.8) | copy-start | bytes 196

commit v3 on v2

--- a/solution.py
+++ b/solution.py
@@ -279,7 +279,7 @@
     )
 
 
-def fill_planes(who_ref, waves_ref, pairs, store):
+def fill_pair(who_ref, waves_ref, pairs, store):
     def fill(k, carry):
         for z in range(STEP_Z):
             home = waves_ref[who_ref[0], z, k].astype(F32)
@@ -291,21 +291,50 @@
             store(pl.ds(pairs * PAIRS + start, PAIRS), lanes, imag_part)
         return carry
 
-    lax.fori_loop(0, pairs, fill, 0)
-
-
-def response_kernel(pairs, who_ref, waves_ref, inter_ref, out_ref, val_ref):
-    def store(rows, lanes, values):
-        val_ref[rows, lanes] = values.astype(BF)
-
-    fill_planes(who_ref, waves_ref, pairs, store)
-
-    @pl.when(pl.program_id(0) == 0)
+    return fill
+
+
+def response_kernel(pairs, who_ref, waves_ref, inter_ref, out_ref, even_ref, odd_ref):
+    step = pl.program_id(0)
+    steps = pl.num_programs(0) - 1
+    width = 256
+    chunks = out_ref.shape[1] // width
+    each = pairs // chunks
+
+    def work(fill_ref, dot_ref):
+        def store(rows, lanes, values):
+            fill_ref[rows, lanes] = values.astype(BF)
+
+        fill = fill_pair(who_ref, waves_ref, pairs, store)
+
+        def run(c, carry):
+            if dot_ref is not None:
+                lanes = pl.ds(pl.multiple_of(c * width, width), width)
+                inter = inter_ref[:, :, lanes].reshape(STEP_Z * NXY, width)
+                out_ref[:, lanes] += jnp.dot(dot_ref[...], inter, preferred_element_type=F32)
+            if fill_ref is not None:
+                for i in range(each):
+                    fill(c * each + i, 0)
+            return carry
+
+        lax.fori_loop(0, chunks, run, 0)
+
+    @pl.when(step == 0)
     def _():
         out_ref[...] = jnp.zeros_like(out_ref)
-
-    inter = inter_ref[...].reshape(STEP_Z * NXY, inter_ref.shape[2])
-    out_ref[...] += jnp.dot(val_ref[...], inter, preferred_element_type=F32)
+        work(even_ref, None)
+
+    @pl.when((step % 2 == 1) & (step < steps))
+    def _():
+        work(odd_ref, even_ref)
+
+    @pl.when((step % 2 == 0) & (step > 0) & (step < steps))
+    def _():
+        work(even_ref, odd_ref)
+
+    @pl.when(step == steps)
+    def _():
+        work(None, odd_ref)
 
 
 def block_kernel(
@@ -329,7 +358,7 @@
         cond_ref[where, lanes] = high
         cond_low_ref[where, lanes] = low
 
-    fill_planes(who_ref, waves_ref, pairs, store)
+    lax.fori_loop(0, pairs, fill_pair(who_ref, waves_ref, pairs, store), 0)
 
     @pl.when(step == 0)
     def _():
@@ -373,24 +402,25 @@
         lax.fori_loop(0, pairs, finish, 0)
 
 
-def waves_spec(waves):
+def waves_spec(waves, last):
     shape = (waves.shape[0], STEP_Z) + waves.shape[2:]
-    return pl.BlockSpec(shape, lambda i, who: (0, i, 0, 0, 0))
+    return pl.BlockSpec(shape, lambda i, who: (0, jnp.minimum(i, last), 0, 0, 0))
 
 
 def all_responses(who, waves, inter):
     pairs = waves.shape[2]
     rows2 = inter.shape[2]
     half2 = 2 * pairs * PAIRS
+    steps = NZ // STEP_Z
     spec = pltpu.PrefetchScalarGridSpec(
         num_scalar_prefetch=1,
-        grid=(NZ // STEP_Z,),
+        grid=(steps + 1,),
         in_specs=[
-            waves_spec(waves),
-            pl.BlockSpec((STEP_Z, NXY, rows2), lambda i, who: (i, 0, 0)),
+            waves_spec(waves, steps - 1),
+            pl.BlockSpec((STEP_Z, NXY, rows2), lambda i, who: (jnp.maximum(i - 1, 0), 0, 0)),
         ],
         out_specs=pl.BlockSpec((half2, rows2), lambda i, who: (0, 0)),
-        scratch_shapes=[pltpu.VMEM((half2, STEP_Z * NXY), BF)],
+        scratch_shapes=[pltpu.VMEM((half2, STEP_Z * NXY), BF)] * 2,
     )
     return pl.pallas_call(
         functools.partial(response_kernel, pairs),
@@ -410,7 +440,7 @@
         num_scalar_prefetch=1,
         grid=(NZ // STEP_Z,),
         in_specs=[
-            waves_spec(waves),
+            waves_spec(waves, NZ // STEP_Z - 1),
             pl.BlockSpec((half2, rows2), lambda i, who: (0, 0)),
             pl.BlockSpec(first.shape, lambda i, who: (0, 0)),
             pl.BlockSpec((1,) + second.shape[1:], lambda i, who: (i, 0, 0)),

time: 190 us -> 192 us (1.011)
  Pallas kernels: 169 us -> 171 us
where the time goes in v3:
time: 192 us; the launch traced here: 190 us
  Pallas kernels  171 us (89%)
  local copies, waits for them, and re-layouts  12.3 us (6%)
  other arithmetic  6.62 us (3%)
    pallas_call x1, Pallas kernels, transformed_interaction(): pl.pallas_call(functools.partial(interaction_kernel, steps, holders, memb...  68 us
    pallas_call x1, Pallas kernels, partial_blocks(): pl.pallas_call(functools.partial(block_kernel, pairs), grid_spec=spec, ou...  41.1 us
    pallas_call x1, Pallas kernels, all_responses(): pl.pallas_call(functools.partial(response_kernel, pairs), grid_spec=spec,...  32.5 us
    pallas_call x1, Pallas kernels, summed_everywhere(): pl.pallas_call(functools.partial(sum_kernel, holders, members), out_shape...  22.7 us
    pallas_call x1, Pallas kernels, mirrored(): pl.pallas_call(mirror_kernel, grid_spec=spec, out_shape=jax.ShapeDtypeStr...  6.47 us

profile of v3, /device:TPU:0, one launch (start us, length us, event | category | flops | bytes accessed | tf_op | source)
XLA Modules:
  0.0 190.4 jit_solution(5541957674370719333)
XLA Ops:
  0.7 1.3 gather_fusion
  2.0 0.6 pad_add_fusion.who_ref
  2.6 1.4 add_select_fusion.1
  4.0 1.2 fusion.20
  5.1 0.7 copy_bitcast_fusion
  5.9 68.0 %shard_map.86 = (bf16[32,256,1024]{2,1,0:T(8,128)(2,1)}, bf16[2,4,4,2,8,16,256]{6,5,4,3,2,1,0:T(8,128)(2,1)}, bf16[2,4,4,2,8,16,256]{6,5,4,3,2,1,0:T(8,128)(2,1)}) custom-call(bf16[64,32]{1,0:T(8,128)(2,1)} %constant.156.clone.line_ref, bf16[512,512]{1,0:T(8,128)(2,1)} %constant.157.clone.plane_ref, s32[16,1,512]{2,1,0:T(1,128)} %bitcast.34, ...), custom_call_target="tpu_custom_call" | custom-call | flops 17179869184 | bytes 25165824 | tf_op jit(solution)/shard_map/pallas_call | solution.py:224
  73.8 0.0 copy-start.1
  73.8 32.5 %shard_map.87.response_ref = f32[1024,1024]{1,0:T(8,128)} custom-call(s32[17]{0:T(128)} %pad_add_fusion.who_ref, bf16[2,32,8,16,256]{4,3,2,1,0:T(8,128)(2,1)} %bitcast.36, bf16[32,256,1024]{2,1,0:T(8,128)(2,1)} %get-tuple-element.7.inter_ref), custom_call_target="tpu_custom_call" | custom-call | flops 17179869184 | bytes 16777216 | tf_op jit(solution)/shard_map/pallas_call | solution.py:425
  106.3 0.2 fusion.12
  106.5 0.0 copy-done.1
  106.5 0.4 multiply_convert_fusion
  106.9 0.3 copy.41
  107.2 1.3 copy.35.first_ref
  108.5 0.8 add_select_fusion.3
  109.3 0.3 sine_multiply_fusion
  109.6 0.1 copy.34
  109.8 2.2 %select_convert_fusion = bf16[32,2,16,2,512]{4,3,2,1,0:T(2,128)(2,1)S(1)} fusion(pred[16,512]{1,0:T(8,128)(4,1)S(1)} %iota_compare_fusion, bf16[32,2,2,512]{3,2,1,0:T(2,128)(2,1)S(1)} %copy.34), kind=kLoop, calls=%fused_computation.1 | loop fusion | flops 1048576 | bytes 2236416 | tf_op jit(solution)/shard_map/convert_element_type | solution.py:614
  112.0 2.7 %convert_element_type.51.second_ref = bf16[4,256,1024]{2,1,0:T(8,128)(2,1)} reshape(bf16[32,2,16,2,512]{4,3,2,1,0:T(2,128)(2,1)S(1)} %select_convert_fusion) | data formatting | bytes 4194304 | tf_op jit(solution)/shard_map/convert_element_type | solution.py:614
  114.7 41.1 %shard_map.88.part_ref = f32[512,128]{1,0:T(8,128)} custom-call(s32[17]{0:T(128)} %pad_add_fusion.who_ref, bf16[2,32,8,16,256]{4,3,2,1,0:T(8,128)(2,1)} %bitcast.35, f32[1024,1024]{1,0:T(8,128)} %shard_map.87.response_ref, bf16[2048,256]{1,0:T(8,128)(2,1)} %copy.35.first_ref, bf16[4,256,1024]{2,1,0:T(8,128)(2,1)} %convert_element_type.51.second_ref), custom_call_target="tpu_custom_call" | custom-call | flops 8589934592 | bytes 4194304 | tf_op jit(solution)/shard_map/pallas_call | solution.py:455
  155.9 0.0 copy-start
  155.9 22.7 %shard_map.89 = f32[2,512,128]{2,1,0:T(8,128)} custom-call(f32[512,128]{1,0:T(8,128)} %shard_map.88.part_ref), custom_call_target="tpu_custom_call" | custom-call | tf_op jit(solution)/shard_map/pallas_call | solution.py:548
  178.5 1.0 constant_dynamic-slice_fusion
  179.5 0.3 reshape.503
  179.9 1.0 reshape.515
  180.9 0.0 copy-done
  180.9 0.7 select_reduce_fusion.source_ref
  181.6 6.5 %shard_map.90 = f32[8,64,128]{2,1,0:T(8,128)} custom-call(s32[8]{0:T(128)} %select_reduce_fusion.source_ref, f32[16,64,128]{2,1,0:T(8,128)} %bitcast.30), custom_call_target="tpu_custom_call" | custom-call | tf_op jit(solution)/shard_map/pallas_call | solution.py:589
  188.1 1.3 reshape.505
  189.4 1.0 reshape.506
  (13 shorter events, 0.2 us)
Async XLA Ops:
  73.8 32.7 %copy-start.1 = (f32[8,8]{0,1:T(8,128)S(1)}, f32[8,8]{0,1:T(8,128)}, u32[]{:S(2)}) copy-start(f32[8,8]{0,1:T(8,128)} %constant.158.clone) | copy-start | bytes 772
  155.9 25.0 %copy-start = (s32[16]{0:T(128)S(1)}, s32[16]{0:T(128)}, u32[]{:S(2)}) copy-start(s32[16]{0:T(128)} %param.8) | copy-start | bytes 196
